TPU v7x, 32 devices: a whole 2x2x4 slice. The times are simulated.
32 devices in a mesh: row: 8 (over y, x, core), tensor: 4 (over z).
Axes of the slice: x: 2, y: 2, z: 4, core: 2. Of those that a mesh axis runs over, the one named last changes fastest.
Arguments:
- hidden_rows: bfloat16 [2048, 8192], P('row'), may hold values from -6 to 6
- w_query: bfloat16 [8192, 8192], P('row', 'tensor'), may hold values from -0.0625 to 0.0625
- w_out: bfloat16 [8192, 8192], P('tensor', 'row'), may hold values from -0.0625 to 0.0625
- pack_key_cache: bfloat16 [65536, 1024], P('row', 'tensor'), may hold values from -250 to 250
- pack_value_cache: bfloat16 [65536, 1024], P('row', 'tensor'), may hold values from -6 to 6
- query_pos: int32 [2048], P('row'), may hold values from 0 to 65535, as said below
- doc_blocks: int32 [8, 4], P('row'), may hold values from 1 to 32, 64 in all within a row
Outputs:
- mixed: bfloat16 [2048, 8192], P('row', 'tensor')
Inputs may be any that keep to these rules, and one draw needn't show every extreme that they name: `query_pos`: each index of row holds 256 consecutive query rows; at most 64 of them lie in any one block of 8192 key positions, and exactly 64 in some blocks. Positions may repeat. `doc_blocks`: each row sums to 64.
All inputs are finite; a program needn't handle non-finite values.
Results may differ from a plain program's by a relative error of at most 0.014.
The roundings to bfloat16 on the way count: a program that leaves them out, or rounds other values in their place, can miss the bound.
Values may be sent and summed in bfloat16 or wider, within the bound.
A program may use at most 192 MiB of HBM per device.

v0:
```python
import math

import jax
import jax.numpy as jnp
from jax import lax
from jax.sharding import PartitionSpec as P

QUERY_HEADS = 64
KEY_VALUE_HEADS = 8
HEAD_SIZE = 128


neg_large = -1e30


def route_slots(positions, key_span, servers):
    target_server = positions // key_span
    server_ids = jnp.arange(servers, dtype=jnp.int32)
    onehot = (target_server[:, None] == server_ids[None, :]).astype(jnp.int32)
    running = jnp.cumsum(onehot, axis=0) - 1
    slot_rank = jnp.sum(onehot * running, axis=1)
    return (target_server, slot_rank)


def body(hidden_rows, w_query, w_out, pack_key_cache, pack_value_cache, query_pos, doc_blocks):
    servers = lax.axis_size("row")
    my_server = lax.axis_index("row")
    row_count = hidden_rows.shape[0]
    key_span = pack_key_cache.shape[0]
    capacity = 2 * row_count // servers
    slot_count = servers * capacity
    head_width = w_query.shape[1]
    kv_local = pack_key_cache.shape[1] // HEAD_SIZE
    heads_per_group = QUERY_HEADS // KEY_VALUE_HEADS
    score_scale = 1.0 / math.sqrt(HEAD_SIZE)
    queries = jnp.dot(
        hidden_rows,
        lax.all_gather(w_query, "row", axis=0, tiled=True),
        preferred_element_type=jnp.float32,
    ).astype(jnp.bfloat16)
    target_server, slot_rank = route_slots(query_pos, key_span, servers)
    slot_index = target_server * capacity + slot_rank
    outgoing = jnp.zeros((slot_count, head_width), jnp.bfloat16).at[slot_index].set(queries)
    incoming = lax.all_to_all(
        outgoing.reshape(servers, capacity, head_width),
        "row",
        split_axis=0,
        concat_axis=0,
        tiled=True,
    )
    every_pos = lax.all_gather(query_pos, "row", axis=0, tiled=True).reshape(servers, row_count)
    src_server, src_rank = jax.vmap(lambda positions: route_slots(positions, key_span, servers))(
        every_pos
    )
    source_base = jnp.arange(servers, dtype=jnp.int32)[:, None] * capacity
    landing = jnp.where(src_server == my_server, source_base + src_rank, slot_count)
    local_offset = every_pos - my_server * key_span
    slot_offset = (
        jnp.full((slot_count + 1,), -1, jnp.int32)
        .at[landing.reshape(-1)]
        .set(local_offset.reshape(-1))[:slot_count]
    )
    doc_ends = jnp.cumsum(doc_blocks[0]) * 128
    key_index = jnp.arange(key_span, dtype=jnp.int32)
    key_doc = jnp.sum((key_index[:, None] >= doc_ends[None, :]).astype(jnp.int32), axis=1)
    slot_doc = jnp.sum((slot_offset[:, None] >= doc_ends[None, :]).astype(jnp.int32), axis=1)
    block_slots = min(64, slot_count)
    block_total = slot_count // block_slots
    key_heads = pack_key_cache.reshape(key_span, kv_local, HEAD_SIZE)
    value_heads = pack_value_cache.reshape(key_span, kv_local, HEAD_SIZE)

    def attend(packed):
        query_blk, offset_blk, doc_blk = packed
        scores = (
            jnp.einsum("sagd,kad->agsk", query_blk, key_heads, preferred_element_type=jnp.float32)
            * score_scale
        )
        allowed = (key_index[None, :] <= offset_blk[:, None]) & (
            key_doc[None, :] == doc_blk[:, None]
        )
        scores = jnp.where(allowed[None, None], scores, neg_large)
        top_score = jnp.max(scores, axis=3, keepdims=True)
        weights = jnp.where(allowed[None, None], jnp.exp(scores - top_score), 0.0)
        sums = jnp.sum(weights, axis=3)
        sums = jnp.where(sums > 0.0, sums, 1.0)
        mixed_heads = jnp.einsum(
            "agsk,kad->sagd",
            weights.astype(jnp.bfloat16),
            value_heads,
            preferred_element_type=jnp.float32,
        )
        divisor = jnp.transpose(sums, (2, 0, 1))[..., None]
        return (mixed_heads / divisor).astype(jnp.bfloat16)

    query_blocks = incoming.reshape(block_total, block_slots, kv_local, heads_per_group, HEAD_SIZE)
    attended = lax.map(
        attend,
        (
            query_blocks,
            slot_offset.reshape(block_total, block_slots),
            slot_doc.reshape(block_total, block_slots),
        ),
    )
    attended = attended.reshape(slot_count, head_width)
    returned = lax.all_to_all(
        attended.reshape(servers, capacity, head_width),
        "row",
        split_axis=0,
        concat_axis=0,
        tiled=True,
    )
    own_rows = returned.reshape(slot_count, head_width)[slot_index]
    return lax.psum_scatter(
        jnp.dot(
            own_rows,
            lax.all_gather(w_out, "row", axis=1, tiled=True),
            preferred_element_type=jnp.float32,
        ).astype(jnp.bfloat16),
        "tensor",
        scatter_dimension=1,
        tiled=True,
    )


def solution(mesh):
    return jax.shard_map(
        body,
        mesh=mesh,
        in_specs=(
            P("row", None),
            P("row", "tensor"),
            P("tensor", "row"),
            P("row", "tensor"),
            P("row", "tensor"),
            P("row"),
            P("row", None),
        ),
        out_specs=P("row", "tensor"),
        check_vma=False,
    )
```

profile of v0, /device:TPU:0, one launch (start us, length us, event | category | flops | bytes accessed | tf_op | source)
XLA Modules:
  0.0 870.0 jit_solution(14625011002217816209)
XLA Ops:
  8.0 10.3 %all-gather = s32[8,1,256]{2,1,0:T(1,128)S(1)} all-gather(s32[1,1,256]{2,1,0:T(1,128)S(1)} %bitcast.148), channel_id=1, replica_groups=mesh['row'=8,'tensor'=4] {'row'}, dimensions={0}, use_global_device_ids=true | all-gather | bytes 9216 | tf_op jit(solution)/shard_map/all_gather | solution.py:51
  19.4 153.4 %all-gather.4.cloned.1.call-done = bf16[8192,2048]{1,0:T(8,128)(2,1)} async-done(((bf16[1024,2048]{1,0:T(8,128)(2,1)}), bf16[8192,2048]{1,0:T(8,128)(2,1)}) %all-gather.4.cloned.1.call-update) | async-done | bytes 33554448 | tf_op jit(solution)/shard_map/all_gather | solution.py:38
  172.8 18.7 %convolution_convert_fusion.1 = bf16[256,2048]{1,0:T(8,128)(2,1)S(1)} fusion(bf16[256,8192]{1,0:T(8,128)(2,1)} %param.9, bf16[8192,2048]{1,0:T(8,128)(2,1)} %all-gather.4.cloned.1.call-done), kind=kOutput, calls=%fused_computation.36 | convolution fusion | flops 8590458880 | bytes 38797312 | tf_op jit(solution)/shard_map/dot_general | solution.py:36
  238.1 10.1 %all-to-all-done = bf16[8,64,2048]{2,1,0:T(8,128)(2,1)S(1)} async-done(((bf16[8,64,2048]{2,1,0:T(8,128)(2,1)}), bf16[8,64,2048]{2,1,0:T(8,128)(2,1)S(1)}, u32[]{:S(2)}, u32[]{:S(2)}) %all-to-all-start) | async-done | bytes 2097184 | tf_op jit(solution)/shard_map/all_to_all | solution.py:44
  250.2 485.3 %while.11 = (s32[]{:T(128)}, bf16[8,64,2,8,128]{4,3,2,1,0:T(8,128)(2,1)}, s32[8,64]{1,0:T(8,128)S(1)}, s32[8192]{0:T(1024)S(1)}, s32[8,64]{1,0:T(8,128)S(1)}, /*...) while((s32[]{:T(128)}, ...), condition=%wide.region_14.15_spmd.clone, body=%wide.region_11.14_spmd.clone.sunk | while | flops 4363921408 | bytes 111200864 | solution.py:96
  250.7 23.4 %fusion.78 = f32[2,64,8,8192]{3,2,1,0:T(8,128)} fusion(bf16[8192,2,128]{2,0,1:T(8,128)(2,1)} %get-tuple-element.200, bf16[8,64,2,8,128]{4,3,2,1,0:T(8,128)(2,1)} %get-tuple-element.199, s32[]{:T(128)} %get-tuple-element.185), kind=kOutput, calls=%fused_computation.17.clone.1 | convolution fusion | flops 2147483648 | bytes 38011392 | tf_op jit(solution)/shard_map/while/body/eval_jaxpr/sagd,kad->agsk/dot_general | solution.py:75
  274.1 31.9 %fusion.81 = (f32[2,8,64]{1,2,0:T(8,128)S(1)}, bf16[2,8,64,8192]{3,1,2,0:T(8,128)(2,1)}) fusion(f32[2,64,8,8192]{3,2,1,0:T(8,128)} %fusion.78, pred[64,8192]{1,0:T(8,128)(4,1)S(1)} %fusion.80), kind=kOutput, calls=%fused_computation.94.clone.1 | output fusion | flops 67117056 | bytes 50860032 | tf_op jit(solution)/shard_map/while/body/eval_jaxpr/sub | solution.py:83
  306.0 9.9 %fusion.82 = bf16[1,64,2,8,128]{4,3,1,2,0:T(8,128)(2,1)S(1)} fusion(bf16[8192,2,128]{2,0,1:T(8,128)(2,1)} %get-tuple-element.201, bf16[2,8,64,8192]{3,1,2,0:T(8,128)(2,1)} %get-tuple-element.174, f32[64,2,8]{2,0,1:T(8,128)S(1)} %compare_select_fusion.4), kind=kOutput, calls=%fused_computation.24.clone.1 | convolution fusion | flops 2147745792 | bytes 21237760 | tf_op jit(solution)/shard_map/while/body/eval_jaxpr/agsk,kad->sagd/dot_general | solution.py:86
  317.1 18.4 %fusion.78 = f32[2,64,8,8192]{3,2,1,0:T(8,128)} fusion(bf16[8192,2,128]{2,0,1:T(8,128)(2,1)} %get-tuple-element.200, bf16[8,64,2,8,128]{4,3,2,1,0:T(8,128)(2,1)} %get-tuple-element.199, s32[]{:T(128)} %get-tuple-element.185), kind=kOutput, calls=%fused_computation.17.clone.1 | convolution fusion | flops 2147483648 | bytes 38011392 | tf_op jit(solution)/shard_map/while/body/eval_jaxpr/sagd,kad->agsk/dot_general | solution.py:75
  335.4 31.8 %fusion.81 = (f32[2,8,64]{1,2,0:T(8,128)S(1)}, bf16[2,8,64,8192]{3,1,2,0:T(8,128)(2,1)}) fusion(f32[2,64,8,8192]{3,2,1,0:T(8,128)} %fusion.78, pred[64,8192]{1,0:T(8,128)(4,1)S(1)} %fusion.80), kind=kOutput, calls=%fused_computation.94.clone.1 | output fusion | flops 67117056 | bytes 50860032 | tf_op jit(solution)/shard_map/while/body/eval_jaxpr/sub | solution.py:83
  367.2 9.3 %fusion.82 = bf16[1,64,2,8,128]{4,3,1,2,0:T(8,128)(2,1)S(1)} fusion(bf16[8192,2,128]{2,0,1:T(8,128)(2,1)} %get-tuple-element.201, bf16[2,8,64,8192]{3,1,2,0:T(8,128)(2,1)} %get-tuple-element.174, f32[64,2,8]{2,0,1:T(8,128)S(1)} %compare_select_fusion.4), kind=kOutput, calls=%fused_computation.24.clone.1 | convolution fusion | flops 2147745792 | bytes 21237760 | tf_op jit(solution)/shard_map/while/body/eval_jaxpr/agsk,kad->sagd/dot_general | solution.py:86
  377.8 17.9 %fusion.78 = f32[2,64,8,8192]{3,2,1,0:T(8,128)} fusion(bf16[8192,2,128]{2,0,1:T(8,128)(2,1)} %get-tuple-element.200, bf16[8,64,2,8,128]{4,3,2,1,0:T(8,128)(2,1)} %get-tuple-element.199, s32[]{:T(128)} %get-tuple-element.185), kind=kOutput, calls=%fused_computation.17.clone.1 | convolution fusion | flops 2147483648 | bytes 38011392 | tf_op jit(solution)/shard_map/while/body/eval_jaxpr/sagd,kad->agsk/dot_general | solution.py:75
  395.7 31.2 %fusion.81 = (f32[2,8,64]{1,2,0:T(8,128)S(1)}, bf16[2,8,64,8192]{3,1,2,0:T(8,128)(2,1)}) fusion(f32[2,64,8,8192]{3,2,1,0:T(8,128)} %fusion.78, pred[64,8192]{1,0:T(8,128)(4,1)S(1)} %fusion.80), kind=kOutput, calls=%fused_computation.94.clone.1 | output fusion | flops 67117056 | bytes 50860032 | tf_op jit(solution)/shard_map/while/body/eval_jaxpr/sub | solution.py:83
  426.9 9.3 %fusion.82 = bf16[1,64,2,8,128]{4,3,1,2,0:T(8,128)(2,1)S(1)} fusion(bf16[8192,2,128]{2,0,1:T(8,128)(2,1)} %get-tuple-element.201, bf16[2,8,64,8192]{3,1,2,0:T(8,128)(2,1)} %get-tuple-element.174, f32[64,2,8]{2,0,1:T(8,128)S(1)} %compare_select_fusion.4), kind=kOutput, calls=%fused_computation.24.clone.1 | convolution fusion | flops 2147745792 | bytes 21237760 | tf_op jit(solution)/shard_map/while/body/eval_jaxpr/agsk,kad->sagd/dot_general | solution.py:86
  437.5 17.9 %fusion.78 = f32[2,64,8,8192]{3,2,1,0:T(8,128)} fusion(bf16[8192,2,128]{2,0,1:T(8,128)(2,1)} %get-tuple-element.200, bf16[8,64,2,8,128]{4,3,2,1,0:T(8,128)(2,1)} %get-tuple-element.199, s32[]{:T(128)} %get-tuple-element.185), kind=kOutput, calls=%fused_computation.17.clone.1 | convolution fusion | flops 2147483648 | bytes 38011392 | tf_op jit(solution)/shard_map/while/body/eval_jaxpr/sagd,kad->agsk/dot_general | solution.py:75
  455.4 31.2 %fusion.81 = (f32[2,8,64]{1,2,0:T(8,128)S(1)}, bf16[2,8,64,8192]{3,1,2,0:T(8,128)(2,1)}) fusion(f32[2,64,8,8192]{3,2,1,0:T(8,128)} %fusion.78, pred[64,8192]{1,0:T(8,128)(4,1)S(1)} %fusion.80), kind=kOutput, calls=%fused_computation.94.clone.1 | output fusion | flops 67117056 | bytes 50860032 | tf_op jit(solution)/shard_map/while/body/eval_jaxpr/sub | solution.py:83
  486.6 9.3 %fusion.82 = bf16[1,64,2,8,128]{4,3,1,2,0:T(8,128)(2,1)S(1)} fusion(bf16[8192,2,128]{2,0,1:T(8,128)(2,1)} %get-tuple-element.201, bf16[2,8,64,8192]{3,1,2,0:T(8,128)(2,1)} %get-tuple-element.174, f32[64,2,8]{2,0,1:T(8,128)S(1)} %compare_select_fusion.4), kind=kOutput, calls=%fused_computation.24.clone.1 | convolution fusion | flops 2147745792 | bytes 21237760 | tf_op jit(solution)/shard_map/while/body/eval_jaxpr/agsk,kad->sagd/dot_general | solution.py:86
  497.2 17.9 %fusion.78 = f32[2,64,8,8192]{3,2,1,0:T(8,128)} fusion(bf16[8192,2,128]{2,0,1:T(8,128)(2,1)} %get-tuple-element.200, bf16[8,64,2,8,128]{4,3,2,1,0:T(8,128)(2,1)} %get-tuple-element.199, s32[]{:T(128)} %get-tuple-element.185), kind=kOutput, calls=%fused_computation.17.clone.1 | convolution fusion | flops 2147483648 | bytes 38011392 | tf_op jit(solution)/shard_map/while/body/eval_jaxpr/sagd,kad->agsk/dot_general | solution.py:75
  515.1 31.2 %fusion.81 = (f32[2,8,64]{1,2,0:T(8,128)S(1)}, bf16[2,8,64,8192]{3,1,2,0:T(8,128)(2,1)}) fusion(f32[2,64,8,8192]{3,2,1,0:T(8,128)} %fusion.78, pred[64,8192]{1,0:T(8,128)(4,1)S(1)} %fusion.80), kind=kOutput, calls=%fused_computation.94.clone.1 | output fusion | flops 67117056 | bytes 50860032 | tf_op jit(solution)/shard_map/while/body/eval_jaxpr/sub | solution.py:83
  546.3 9.3 %fusion.82 = bf16[1,64,2,8,128]{4,3,1,2,0:T(8,128)(2,1)S(1)} fusion(bf16[8192,2,128]{2,0,1:T(8,128)(2,1)} %get-tuple-element.201, bf16[2,8,64,8192]{3,1,2,0:T(8,128)(2,1)} %get-tuple-element.174, f32[64,2,8]{2,0,1:T(8,128)S(1)} %compare_select_fusion.4), kind=kOutput, calls=%fused_computation.24.clone.1 | convolution fusion | flops 2147745792 | bytes 21237760 | tf_op jit(solution)/shard_map/while/body/eval_jaxpr/agsk,kad->sagd/dot_general | solution.py:86
  556.9 17.9 %fusion.78 = f32[2,64,8,8192]{3,2,1,0:T(8,128)} fusion(bf16[8192,2,128]{2,0,1:T(8,128)(2,1)} %get-tuple-element.200, bf16[8,64,2,8,128]{4,3,2,1,0:T(8,128)(2,1)} %get-tuple-element.199, s32[]{:T(128)} %get-tuple-element.185), kind=kOutput, calls=%fused_computation.17.clone.1 | convolution fusion | flops 2147483648 | bytes 38011392 | tf_op jit(solution)/shard_map/while/body/eval_jaxpr/sagd,kad->agsk/dot_general | solution.py:75
  574.8 31.2 %fusion.81 = (f32[2,8,64]{1,2,0:T(8,128)S(1)}, bf16[2,8,64,8192]{3,1,2,0:T(8,128)(2,1)}) fusion(f32[2,64,8,8192]{3,2,1,0:T(8,128)} %fusion.78, pred[64,8192]{1,0:T(8,128)(4,1)S(1)} %fusion.80), kind=kOutput, calls=%fused_computation.94.clone.1 | output fusion | flops 67117056 | bytes 50860032 | tf_op jit(solution)/shard_map/while/body/eval_jaxpr/sub | solution.py:83
  606.0 9.3 %fusion.82 = bf16[1,64,2,8,128]{4,3,1,2,0:T(8,128)(2,1)S(1)} fusion(bf16[8192,2,128]{2,0,1:T(8,128)(2,1)} %get-tuple-element.201, bf16[2,8,64,8192]{3,1,2,0:T(8,128)(2,1)} %get-tuple-element.174, f32[64,2,8]{2,0,1:T(8,128)S(1)} %compare_select_fusion.4), kind=kOutput, calls=%fused_computation.24.clone.1 | convolution fusion | flops 2147745792 | bytes 21237760 | tf_op jit(solution)/shard_map/while/body/eval_jaxpr/agsk,kad->sagd/dot_general | solution.py:86
  616.6 17.9 %fusion.78 = f32[2,64,8,8192]{3,2,1,0:T(8,128)} fusion(bf16[8192,2,128]{2,0,1:T(8,128)(2,1)} %get-tuple-element.200, bf16[8,64,2,8,128]{4,3,2,1,0:T(8,128)(2,1)} %get-tuple-element.199, s32[]{:T(128)} %get-tuple-element.185), kind=kOutput, calls=%fused_computation.17.clone.1 | convolution fusion | flops 2147483648 | bytes 38011392 | tf_op jit(solution)/shard_map/while/body/eval_jaxpr/sagd,kad->agsk/dot_general | solution.py:75
  634.4 31.2 %fusion.81 = (f32[2,8,64]{1,2,0:T(8,128)S(1)}, bf16[2,8,64,8192]{3,1,2,0:T(8,128)(2,1)}) fusion(f32[2,64,8,8192]{3,2,1,0:T(8,128)} %fusion.78, pred[64,8192]{1,0:T(8,128)(4,1)S(1)} %fusion.80), kind=kOutput, calls=%fused_computation.94.clone.1 | output fusion | flops 67117056 | bytes 50860032 | tf_op jit(solution)/shard_map/while/body/eval_jaxpr/sub | solution.py:83
  665.7 9.3 %fusion.82 = bf16[1,64,2,8,128]{4,3,1,2,0:T(8,128)(2,1)S(1)} fusion(bf16[8192,2,128]{2,0,1:T(8,128)(2,1)} %get-tuple-element.201, bf16[2,8,64,8192]{3,1,2,0:T(8,128)(2,1)} %get-tuple-element.174, f32[64,2,8]{2,0,1:T(8,128)S(1)} %compare_select_fusion.4), kind=kOutput, calls=%fused_computation.24.clone.1 | convolution fusion | flops 2147745792 | bytes 21237760 | tf_op jit(solution)/shard_map/while/body/eval_jaxpr/agsk,kad->sagd/dot_general | solution.py:86
  676.3 17.9 %fusion.78 = f32[2,64,8,8192]{3,2,1,0:T(8,128)} fusion(bf16[8192,2,128]{2,0,1:T(8,128)(2,1)} %get-tuple-element.200, bf16[8,64,2,8,128]{4,3,2,1,0:T(8,128)(2,1)} %get-tuple-element.199, s32[]{:T(128)} %get-tuple-element.185), kind=kOutput, calls=%fused_computation.17.clone.1 | convolution fusion | flops 2147483648 | bytes 38011392 | tf_op jit(solution)/shard_map/while/body/eval_jaxpr/sagd,kad->agsk/dot_general | solution.py:75
  694.1 31.2 %fusion.81 = (f32[2,8,64]{1,2,0:T(8,128)S(1)}, bf16[2,8,64,8192]{3,1,2,0:T(8,128)(2,1)}) fusion(f32[2,64,8,8192]{3,2,1,0:T(8,128)} %fusion.78, pred[64,8192]{1,0:T(8,128)(4,1)S(1)} %fusion.80), kind=kOutput, calls=%fused_computation.94.clone.1 | output fusion | flops 67117056 | bytes 50860032 | tf_op jit(solution)/shard_map/while/body/eval_jaxpr/sub | solution.py:83
  725.4 9.3 %fusion.82 = bf16[1,64,2,8,128]{4,3,1,2,0:T(8,128)(2,1)S(1)} fusion(bf16[8192,2,128]{2,0,1:T(8,128)(2,1)} %get-tuple-element.201, bf16[2,8,64,8192]{3,1,2,0:T(8,128)(2,1)} %get-tuple-element.174, f32[64,2,8]{2,0,1:T(8,128)S(1)} %compare_select_fusion.4), kind=kOutput, calls=%fused_computation.24.clone.1 | convolution fusion | flops 2147745792 | bytes 21237760 | tf_op jit(solution)/shard_map/while/body/eval_jaxpr/agsk,kad->sagd/dot_general | solution.py:86
  743.3 26.5 %all-to-all-done.1 = bf16[8,64,2048]{2,1,0:T(8,128)(2,1)S(1)} async-done(((bf16[8,64,2048]{2,1,0:T(8,128)(2,1)}), bf16[8,64,2048]{2,1,0:T(8,128)(2,1)S(1)}, u32[]{:S(2)}, u32[]{:S(2)}) %all-to-all-start.1) | async-done | bytes 2097184 | tf_op jit(solution)/shard_map/all_to_all | solution.py:105
  771.2 16.4 %convolution_convert_fusion = bf16[256,8192]{1,0:T(8,128)(2,1)} fusion(bf16[256,2048]{1,0:T(8,128)(2,1)S(1)} %gather_fusion, bf16[2048,8192]{1,0:T(8,128)(2,1)} %all-gather.6.cloned.1.call-done), kind=kOutput, calls=%fused_computation.35 | convolution fusion | flops 8592031744 | bytes 38797312 | tf_op jit(solution)/shard_map/dot_general | solution.py:114
  787.6 75.8 %reduce-scatter.2.cloned.1.call-done = bf16[256,2048]{1,0:T(8,128)(2,1)} async-done(((bf16[256,8192]{1,0:T(8,128)(2,1)}), bf16[256,2048]{1,0:T(8,128)(2,1)}) %reduce-scatter.2.cloned.1.call-update) | async-done | bytes 1048592 | tf_op jit(solution)/shard_map/reduce_scatter | solution.py:113
  (91 shorter events, 70.0 us)
Async XLA Ops:
  6.5 1.5 copy-start
  6.5 166.2 %all-gather.4.cloned.1.call-start = ((), (), s32[]{:S(2)}) async-start(), calls=%async_computation.3 | async-start | bytes 37748736 | tf_op jit(solution)/shard_map/all_gather | solution.py:38
  7.3 764.0 %all-gather.6.cloned.1.call-start = ((), (), s32[]{:S(2)}) async-start(), calls=%async_computation.4 | async-start | bytes 37748736 | tf_op jit(solution)/shard_map/all_gather | solution.py:116
  19.3 172.2 %copy-start.1 = (s32[256]{0:T(256)}, s32[256]{0:T(256)S(1)}, u32[]{:S(2)}) copy-start(s32[256]{0:T(256)S(1)} %compare_select_fusion.2) | copy-start | bytes 3076
  191.5 20.6 %copy-start.3 = (s32[1,4]{1,0:T(1,128)S(1)}, s32[1,4]{1,0:T(1,128)}, u32[]{:S(2)}) copy-start(s32[1,4]{1,0:T(1,128)} %param.15) | copy-start | bytes 52
  195.3 52.9 %all-to-all-start = ((bf16[8,64,2048]{2,1,0:T(8,128)(2,1)}), bf16[8,64,2048]{2,1,0:T(8,128)(2,1)S(1)}, u32[]{:S(2)}, u32[]{:S(2)}) async-start(bf16[8,64,2048]{2,1,0:T(8,128)(2,1)} %bitcast.144), calls=%async_computation | async-start | bytes 4194304 | tf_op jit(solution)/shard_map/all_to_all | solution.py:44
  735.5 7.8 copy-start.2
  739.7 30.2 %all-to-all-start.1 = ((bf16[8,64,2048]{2,1,0:T(8,128)(2,1)}), bf16[8,64,2048]{2,1,0:T(8,128)(2,1)S(1)}, u32[]{:S(2)}, u32[]{:S(2)}) async-start(bf16[8,64,2048]{2,1,0:T(8,128)(2,1)} %reshape_reshape.3), calls=%async_computation.1 | async-start | bytes 4194304 | tf_op jit(solution)/shard_map/all_to_all | solution.py:105
  743.3 120.2 %reduce-scatter.2.cloned.1.call-start = ((), (), s32[]{:S(2)}) async-start(), calls=%async_computation.5 | async-start | bytes 5242880 | tf_op jit(solution)/shard_map/reduce_scatter | solution.py:113
Sparse Core Ops, SparseCore 0:
  9.2 163.4 all-gather.3
  174.7 183.2 all-gather.5
  787.7 75.6 reduce-scatter.1
where the time goes:
time: 871 us; the launch traced here: 870 us
  waiting for transfers between devices  267 us (31%)
  other arithmetic  261 us (30%)
  matrix products  259 us (30%)
  local copies, waits for them, and re-layouts  51.4 us (6%)
  between operations  13.3 us (2%)
  blocking collectives  10.3 us (1%)
    sub x8, other arithmetic, attend(): weights = jnp.where(allowed[None, None], jnp.exp(scores - top_score), 0.0)  251 us
    all_gather x1, waiting for transfers between devices, body(): lax.all_gather(w_query, 'row', axis=0, tiled=True)  153 us
    dot_general x8, matrix products, attend(): jnp.einsum('sagd,kad->agsk', query_blk, key_heads, preferred_element_type...  149 us
    reduce_scatter x1, waiting for transfers between devices, body(): lax.psum_scatter(jnp.dot(own_rows, lax.all_gather(w_out, 'row', axis=1, t...  75.8 us
    dot_general x8, matrix products, attend(): jnp.einsum('agsk,kad->sagd', weights.astype(jnp.bfloat16), value_heads, p...  75.2 us
    unnamed x14, local copies, waits for them, and re-layouts  27.4 us
    all_to_all x1, waiting for transfers between devices, body(): lax.all_to_all(attended.reshape(servers, capacity, head_width), 'row', sp...  26.5 us
    dot_general x1, matrix products, body(): jnp.dot(hidden_rows, lax.all_gather(w_query, 'row', axis=0, tiled=True),...  18.7 us
  transfers between devices with their start and end apart: 5, of which 4 were waited for; matrix products, arithmetic and copies ran while one was open for 64% of the time, Pallas kernels for 0%

commit v1 on v0

v1 whole, which is shorter than its diff:
```python
import math

import jax
import jax.numpy as jnp
from jax import lax
from jax.experimental import pallas as pl
from jax.experimental.pallas import tpu as pltpu
from jax.sharding import PartitionSpec as P

QUERY_HEADS = 64
KEY_VALUE_HEADS = 8
HEAD_SIZE = 128
HEADS_PER_GROUP = QUERY_HEADS // KEY_VALUE_HEADS
LANES = 128
SLOT_TILE = 32
KEY_TILE = 512
QUERY_CHUNKS = 2
OUT_CHUNKS = 4

neg_large = -1e30


def attend_kernel(lo_ref, hi_ref, q_ref, k_ref, v_ref, off_ref, start_ref, o_ref, s_ref):
    slots = q_ref.shape[0]
    kv_local = k_ref.shape[1] // HEAD_SIZE
    tile = SLOT_TILE
    rows = HEADS_PER_GROUP * tile
    span = s_ref.shape[3]
    factor = math.log2(math.e) / math.sqrt(HEAD_SIZE)

    def head_cols(a, g):
        return pl.ds((a * HEADS_PER_GROUP + g) * HEAD_SIZE, HEAD_SIZE)

    def one_tile(i, carry):
        here = pl.ds(pl.multiple_of(i * tile, tile), tile)
        lo, hi = lo_ref[i], hi_ref[i]
        off = off_ref[here, :]
        start = start_ref[here, :]
        queries = [
            jnp.concatenate([q_ref[here, head_cols(a, g)] for g in range(HEADS_PER_GROUP)], axis=0)
            for a in range(kv_local)
        ]

        def score(kb, tops):
            base = pl.multiple_of(kb * span, span)
            key_index = base + lax.broadcasted_iota(jnp.int32, (tile, span), 1)
            allowed = ((key_index >= start) & (key_index <= off))[None]
            new = []
            for a in range(kv_local):
                keys = k_ref[pl.ds(base, span), pl.ds(a * HEAD_SIZE, HEAD_SIZE)]
                s = lax.dot_general(
                    queries[a], keys, (((1,), (1,)), ((), ())), preferred_element_type=jnp.float32
                )
                s = jnp.where(allowed, s.reshape(HEADS_PER_GROUP, tile, span), neg_large)
                s = s.reshape(rows, span)
                s_ref[kb, a] = s
                top = tops[a]
                for c in range(span // LANES):
                    top = jnp.maximum(top, s[:, c * LANES : (c + 1) * LANES])
                new.append(top)
            return tuple(new)

        tops = lax.fori_loop(
            lo, hi, score, (jnp.full((rows, LANES), neg_large, jnp.float32),) * kv_local
        )
        tops = [jnp.max(top, axis=1, keepdims=True) for top in tops]

        def mix(kb, carry):
            base = pl.multiple_of(kb * span, span)
            new = []
            for a in range(kv_local):
                sums, total = carry[a]
                weights = jnp.exp2((s_ref[kb, a] - tops[a]) * factor)
                for c in range(span // LANES):
                    sums = sums + weights[:, c * LANES : (c + 1) * LANES]
                values = v_ref[pl.ds(base, span), pl.ds(a * HEAD_SIZE, HEAD_SIZE)]
                total = total + jnp.dot(
                    weights.astype(jnp.bfloat16), values, preferred_element_type=jnp.float32
                )
                new.append((sums, total))
            return tuple(new)

        zeros = (jnp.zeros((rows, LANES), jnp.float32), jnp.zeros((rows, HEAD_SIZE), jnp.float32))
        mixed = lax.fori_loop(lo, hi, mix, (zeros,) * kv_local)
        for a in range(kv_local):
            sums, total = mixed[a]
            sums = jnp.sum(sums, axis=1, keepdims=True)
            out = (total / jnp.where(sums > 0.0, sums, 1.0)).astype(jnp.bfloat16)
            for g in range(HEADS_PER_GROUP):
                o_ref[here, head_cols(a, g)] = out[g * tile : (g + 1) * tile]
        return carry

    lax.fori_loop(0, slots // tile, one_tile, 0)


def attend(queries, keys, values, offsets, starts, valid):
    slots, width = queries.shape
    key_span = keys.shape[0]
    kv_local = keys.shape[1] // HEAD_SIZE
    span = min(KEY_TILE, key_span)
    tiles = slots // SLOT_TILE
    by_tile = lambda x: x.reshape(tiles, SLOT_TILE)
    lo = jnp.min(by_tile(jnp.where(valid, starts, key_span)), axis=1)
    hi = jnp.max(by_tile(jnp.where(valid, offsets, -1)), axis=1)
    some = hi >= 0
    lo = jnp.where(some, lo // span, 0)
    hi = jnp.where(some, hi // span + 1, 0)
    vmem = pl.BlockSpec(memory_space=pltpu.VMEM)
    smem = pl.BlockSpec(memory_space=pltpu.SMEM)
    rows = HEADS_PER_GROUP * SLOT_TILE
    return pl.pallas_call(
        attend_kernel,
        out_shape=jax.ShapeDtypeStruct((slots, width), jnp.bfloat16),
        in_specs=[smem, smem, vmem, vmem, vmem, vmem, vmem],
        out_specs=vmem,
        scratch_shapes=[pltpu.VMEM((key_span // span, kv_local, rows, span), jnp.float32)],
        compiler_params=pltpu.CompilerParams(vmem_limit_bytes=52 * 2**20),
        cost_estimate=pl.CostEstimate(
            flops=slots * width * key_span,
            bytes_accessed=4 * slots * width + 4 * key_span * keys.shape[1],
            transcendentals=slots * width * key_span // HEAD_SIZE // 4,
        ),
        name="attend",
    )(lo, hi, queries, keys, values, offsets[:, None], starts[:, None])


def exact_pick(selection, table):
    return jnp.dot(
        selection.astype(jnp.bfloat16), table, preferred_element_type=jnp.float32
    ).astype(jnp.bfloat16)


def body(hidden_rows, w_query, w_out, pack_key_cache, pack_value_cache, query_pos, doc_blocks):
    servers = lax.axis_size("row")
    groups = lax.axis_size("tensor")
    row_count = hidden_rows.shape[0]
    key_span = pack_key_cache.shape[0]
    capacity = 2 * row_count // servers
    slot_count = servers * capacity
    head_width = w_query.shape[1]

    target = query_pos // key_span
    row_index = jnp.arange(row_count, dtype=jnp.int32)
    earlier = (target[:, None] == target[None, :]) & (row_index[None, :] < row_index[:, None])
    slot_index = target * capacity + jnp.sum(earlier.astype(jnp.int32), axis=1)
    slot_ids = jnp.arange(slot_count, dtype=jnp.int32)
    route = slot_ids[:, None] == slot_index[None, :]
    local = query_pos - target * key_span
    out_offset = jnp.sum(jnp.where(route, local[None, :] + 1, 0), axis=1) - 1
    offsets = lax.all_to_all(
        out_offset.reshape(servers, capacity), "row", split_axis=0, concat_axis=0, tiled=True
    ).reshape(slot_count)

    sort_key = jnp.where(offsets >= 0, offsets, key_span) * slot_count + slot_ids
    place = jnp.sum((sort_key[None, :] < sort_key[:, None]).astype(jnp.int32), axis=1)
    order = slot_ids[:, None] == place[None, :]
    sorted_offsets = jnp.sum(jnp.where(order, offsets[None, :] + 1, 0), axis=1) - 1
    doc_ends = jnp.cumsum(doc_blocks[0]) * 128
    starts = jnp.max(
        jnp.where(doc_ends[None, :] <= sorted_offsets[:, None], doc_ends[None, :], 0), axis=1
    )
    valid = sorted_offsets >= 0

    query_parts = []
    step = head_width // QUERY_CHUNKS
    gathered = None
    for c in range(QUERY_CHUNKS):
        part = w_query[:, c * step : (c + 1) * step]
        if gathered is not None:
            part, gathered = lax.optimization_barrier((part, gathered))
            query_parts.append(
                jnp.dot(hidden_rows, gathered, preferred_element_type=jnp.float32).astype(
                    jnp.bfloat16
                )
            )
        gathered = lax.all_gather(part, "row", axis=0, tiled=True)
    out_parts = []
    out_step = w_out.shape[1] // OUT_CHUNKS
    for c in range(OUT_CHUNKS):
        part = w_out[:, c * out_step : (c + 1) * out_step]
        if c == 0:
            part, gathered = lax.optimization_barrier((part, gathered))
            query_parts.append(
                jnp.dot(hidden_rows, gathered, preferred_element_type=jnp.float32).astype(
                    jnp.bfloat16
                )
            )
        else:
            part, out_parts[-1] = lax.optimization_barrier((part, out_parts[-1]))
        out_parts.append(lax.all_gather(part, "row", axis=1, tiled=True))

    queries = jnp.concatenate(query_parts, axis=1)
    outgoing = exact_pick(route, queries)
    incoming = lax.all_to_all(
        outgoing.reshape(servers, capacity, head_width),
        "row",
        split_axis=0,
        concat_axis=0,
        tiled=True,
    ).reshape(slot_count, head_width)
    sorted_queries = exact_pick(order, incoming)
    attended = attend(
        sorted_queries, pack_key_cache, pack_value_cache, sorted_offsets, starts, valid
    )
    attended = exact_pick(order.T, attended)
    returned = lax.all_to_all(
        attended.reshape(servers, capacity, head_width),
        "row",
        split_axis=0,
        concat_axis=0,
        tiled=True,
    ).reshape(slot_count, head_width)
    own_rows = exact_pick(route.T, returned)

    pieces = []
    shares = servers // groups
    for c in range(OUT_CHUNKS):
        partial = jnp.dot(
            own_rows, out_parts[c], preferred_element_type=jnp.float32
        ).astype(jnp.bfloat16)
        partial = jnp.stack(jnp.split(partial, groups, axis=1))
        shared = lax.all_to_all(partial, "tensor", split_axis=0, concat_axis=0, tiled=True)
        piece = jnp.sum(shared.astype(jnp.float32), axis=0).astype(jnp.bfloat16)
        pieces.append(piece.reshape(row_count, shares, out_step))
    return jnp.stack(pieces, axis=2).reshape(row_count, shares * w_out.shape[1])


def solution(mesh):
    return jax.shard_map(
        body,
        mesh=mesh,
        in_specs=(
            P("row", None),
            P("row", "tensor"),
            P("tensor", "row"),
            P("row", "tensor"),
            P("row", "tensor"),
            P("row"),
            P("row", None),
        ),
        out_specs=P("row", "tensor"),
        check_vma=False,
    )
```

time: 871 us -> 660 us (0.76)
  other arithmetic: 261 us -> 8.68 us
  matrix products: 259 us -> 49.1 us
  waiting for transfers between devices: 267 us -> 475 us
  Pallas kernels: 0 us -> 44.5 us
  local copies, waits for them, and re-layouts: 51.4 us -> 13 us
  blocking collectives: 10.3 us -> 30 us
  starting transfers between devices: 7.29 us -> 23.7 us
    sub x9 -> x2, other arithmetic: 251 us -> 0.01 us  [the longest x1 0.01 us: body(): out_offset = jnp.sum(jnp.where(route, local[None, :] + 1, 0), axis=1) - 1]
    dot_general x18 -> x10, matrix products: 259 us -> 49.1 us  [the longest x2 21 us: body(): jnp.dot(hidden_rows, gathered, preferred_element_type=jnp.float32)]
    all_gather x2 -> x6, waiting for transfers between devices: 153 us -> 353 us  [the longest x2 180 us: body(): gathered = lax.all_gather(part, 'row', axis=0, tiled=True)]
    reduce_scatter x1 -> x0, waiting for transfers between devices: 75.8 us -> none  [body(): lax.psum_scatter(jnp.dot(own_rows, lax.all_gather(w_out, 'row', axis=1, t...]
    all_to_all x1 -> x5, waiting for transfers between devices: 26.5 us -> 78.2 us  [the longest x4 78.2 us: body(): lax.all_to_all(partial, 'tensor', split_axis=0, concat_axis=0, tiled=True)]
    pallas_call x0 -> x1, Pallas kernels: none -> 44.5 us  [attend(): pl.pallas_call(attend_kernel, out_shape=jax.ShapeDtypeStruct((slots, widt...]
    all_to_all x1, waiting for transfers between devices: 10.1 us -> 43.2 us  [body(): lax.all_to_all(outgoing.reshape(servers, capacity, head_width), 'row', sp...]
    all_to_all x0 -> x1, blocking collectives: none -> 30 us  [body(): lax.all_to_all(attended.reshape(servers, capacity, head_width), 'row', sp...]
  transfers between devices with their start and end apart: 5 -> 12, of which waited for: 4 -> 10; matrix products, arithmetic and copies ran while one was open for 64% -> 10% of each run, Pallas kernels for 0% -> 7%
where the time goes in v1:
time: 660 us; the launch traced here: 658 us
  waiting for transfers between devices  475 us (72%)
  matrix products  49.1 us (7%)
  Pallas kernels  44.5 us (7%)
  blocking collectives  30 us (5%)
  starting transfers between devices  23.7 us (4%)
  between operations  13.8 us (2%)
  local copies, waits for them, and re-layouts  13 us (2%)
  other arithmetic  8.68 us (1%)
    all_gather x2, waiting for transfers between devices, body(): gathered = lax.all_gather(part, 'row', axis=0, tiled=True)  180 us
    all_gather x4, waiting for transfers between devices, body(): out_parts.append(lax.all_gather(part, 'row', axis=1, tiled=True))  173 us
    all_to_all x4, waiting for transfers between devices, body(): lax.all_to_all(partial, 'tensor', split_axis=0, concat_axis=0, tiled=True)  78.2 us
    pallas_call x1, Pallas kernels, attend(): pl.pallas_call(attend_kernel, out_shape=jax.ShapeDtypeStruct((slots, widt...  44.5 us
    all_to_all x1, waiting for transfers between devices, body(): lax.all_to_all(outgoing.reshape(servers, capacity, head_width), 'row', sp...  43.2 us
    all_to_all x1, blocking collectives, body(): lax.all_to_all(attended.reshape(servers, capacity, head_width), 'row', sp...  30 us
    dot_general x2, matrix products, body(): jnp.dot(hidden_rows, gathered, preferred_element_type=jnp.float32)  21 us
    dot_general x4, matrix products, body(): jnp.dot(own_rows, out_parts[c], preferred_element_type=jnp.float32)  19.8 us
  transfers between devices with their start and end apart: 12, of which 10 were waited for; matrix products, arithmetic and copies ran while one was open for 10% of the time, Pallas kernels for 7%

profile of v1, /device:TPU:0, one launch (start us, length us, event | category | flops | bytes accessed | tf_op | source)
XLA Modules:
  0.0 657.5 jit_solution(1219252198175415431)
XLA Ops:
  6.5 4.6 fusion.16
  11.2 92.7 %all-gather.7.cloned.1.call-done = bf16[8192,1024]{1,0:T(8,128)(2,1)} async-done(((bf16[1024,1024]{1,0:T(8,128)(2,1)}), bf16[8192,1024]{1,0:T(8,128)(2,1)}) %all-gather.7.cloned.1.call-update) | async-done | bytes 16777232 | tf_op jit(solution)/shard_map/all_gather | solution.py:176
  104.0 4.3 fusion.15
  108.3 87.4 %all-gather.9.cloned.1.call-done = bf16[8192,1024]{1,0:T(8,128)(2,1)} async-done(((bf16[1024,1024]{1,0:T(8,128)(2,1)}), bf16[8192,1024]{1,0:T(8,128)(2,1)}) %all-gather.9.cloned.1.call-update) | async-done | bytes 16777232 | tf_op jit(solution)/shard_map/all_gather | solution.py:176
  195.8 57.8 %all-gather.11.cloned.1.call-done = bf16[2048,2048]{1,0:T(8,128)(2,1)} async-done(((bf16[2048,256]{1,0:T(8,128)(2,1)}), bf16[2048,2048]{1,0:T(8,128)(2,1)}) %all-gather.11.cloned.1.call-update) | async-done | bytes 8388624 | tf_op jit(solution)/shard_map/all_gather | solution.py:190
  253.6 57.7 %all-gather.13.cloned.1.call-done = bf16[2048,2048]{1,0:T(8,128)(2,1)} async-done(((bf16[2048,256]{1,0:T(8,128)(2,1)}), bf16[2048,2048]{1,0:T(8,128)(2,1)}) %all-gather.13.cloned.1.call-update) | async-done | bytes 8388624 | tf_op jit(solution)/shard_map/all_gather | solution.py:190
  311.4 57.6 %all-gather.15.cloned.1.call-done = bf16[2048,2048]{1,0:T(8,128)(2,1)} async-done(((bf16[2048,256]{1,0:T(8,128)(2,1)}), bf16[2048,2048]{1,0:T(8,128)(2,1)}) %all-gather.15.cloned.1.call-update) | async-done | bytes 8388624 | tf_op jit(solution)/shard_map/all_gather | solution.py:190
  370.1 3.3 all-to-all-start
  373.4 12.6 %fusion = bf16[256,1024]{0,1:T(8,128)(2,1)S(1)} fusion(bf16[8192,1024]{1,0:T(8,128)(2,1)} %all-gather.7.cloned.1.call-done, bf16[256,8192]{1,0:T(8,128)(2,1)} %param.7), kind=kOutput, calls=%fused_computation.10 | convolution fusion | flops 4295229440 | bytes 21495808 | tf_op jit(solution)/shard_map/dot_general | solution.py:172
  386.0 8.4 %fusion.1 = bf16[256,1024]{0,1:T(8,128)(2,1)S(1)} fusion(bf16[8192,1024]{1,0:T(8,128)(2,1)} %all-gather.9.cloned.1.call-done, bf16[256,8192]{1,0:T(8,128)(2,1)S(1)} %copy-done.2), kind=kOutput, calls=%fused_computation.11 | convolution fusion | flops 4295229440 | bytes 21495808 | tf_op jit(solution)/shard_map/dot_general | solution.py:184
  394.4 2.1 convolution_convert_fusion
  396.5 4.1 all-to-all-start.1
  403.3 43.2 %all-to-all-done.1 = bf16[8,64,2048]{2,1,0:T(8,128)(2,1)S(1)} async-done(((bf16[8,64,2048]{2,1,0:T(8,128)(2,1)}), bf16[8,64,2048]{2,1,0:T(8,128)(2,1)S(1)}, u32[]{:S(2)}, u32[]{:S(2)}) %all-to-all-start.1) | async-done | bytes 2097184 | tf_op jit(solution)/shard_map/all_to_all | solution.py:194
  446.5 2.6 convolution_convert_fusion.2.q_ref
  449.1 44.5 %attend.1 = bf16[512,2048]{1,0:T(8,128)(2,1)} custom-call(s32[16]{0:T(128)S(1)} %get-tuple-element.54.lo_ref, s32[16]{0:T(128)S(1)} %get-tuple-element.53.hi_ref, bf16[512,2048]{1,0:T(8,128)(2,1)} %convolution_convert_fusion.2.q_ref, bf16[8192,256]{1,0:T(8,128)(2,1)} %k_ref.1, bf16[8192,256]{1,0:T(8,128)(2,1)} %v_ref.1, s32[512,1]{1,0:T(8,128)S(1)} %copy.22.off_ref, ...), custom_call_target="tpu_custom_call" | custom-call | flops 8589934592 | bytes 12582912 | tf_op jit(solution)/shard_map/attend/pallas_call | solution.py:111
  493.6 2.9 convolution_convert_fusion.1
  496.5 30.0 %all_to_all.36 = bf16[8,64,2048]{2,1,0:T(8,128)(2,1)S(1)} all-to-all(bf16[8,64,2048]{2,1,0:T(8,128)(2,1)S(1)} %bitcast.68), channel_id=1, replica_groups=mesh['row'=8,'tensor'=4] {'row'}, dimensions={0} | all-to-all | bytes 4194304 | tf_op jit(solution)/shard_map/all_to_all | solution.py:206
  527.3 2.3 convolution_convert_fusion.7
  529.7 1.2 pad_maximum_fusion
  530.8 4.6 all-to-all-start.3
  535.4 5.7 convolution_convert_fusion.6
  542.3 18.2 %all-to-all-done.3 = bf16[4,256,512]{2,1,0:T(8,128)(2,1)S(1)} async-done(((bf16[4,256,512]{2,1,0:T(8,128)(2,1)}), bf16[4,256,512]{2,1,0:T(8,128)(2,1)S(1)}, u32[]{:S(2)}, u32[]{:S(2)}) %all-to-all-start.3) | async-done | bytes 1048608 | tf_op jit(solution)/shard_map/all_to_all | solution.py:222
  560.5 3.5 all-to-all-start.4
  564.0 5.7 convolution_convert_fusion.5
  570.9 18.3 %all-to-all-done.4 = bf16[4,256,512]{2,1,0:T(8,128)(2,1)S(1)} async-done(((bf16[4,256,512]{2,1,0:T(8,128)(2,1)}), bf16[4,256,512]{2,1,0:T(8,128)(2,1)S(1)}, u32[]{:S(2)}, u32[]{:S(2)}) %all-to-all-start.4) | async-done | bytes 1048608 | tf_op jit(solution)/shard_map/all_to_all | solution.py:222
  589.2 3.7 all-to-all-start.5
  593.0 6.0 convolution_convert_fusion.4
  600.2 17.7 %all-to-all-done.5 = bf16[4,256,512]{2,1,0:T(8,128)(2,1)S(1)} async-done(((bf16[4,256,512]{2,1,0:T(8,128)(2,1)}), bf16[4,256,512]{2,1,0:T(8,128)(2,1)S(1)}, u32[]{:S(2)}, u32[]{:S(2)}) %all-to-all-start.5) | async-done | bytes 1048608 | tf_op jit(solution)/shard_map/all_to_all | solution.py:222
  617.9 4.2 all-to-all-start.6
  623.3 24.1 %all-to-all-done.6 = bf16[4,256,512]{2,1,0:T(8,128)(2,1)} async-done(((bf16[4,256,512]{2,1,0:T(8,128)(2,1)}), bf16[4,256,512]{2,1,0:T(8,128)(2,1)}, u32[]{:S(2)}, u32[]{:S(2)}) %all-to-all-start.6) | async-done | bytes 1048608 | tf_op jit(solution)/shard_map/all_to_all | solution.py:222
  647.4 1.5 reduce_sum.91
  649.3 1.4 copy.29
  (66 shorter events, 9.8 us)
Async XLA Ops:
  6.5 97.4 %all-gather.7.cloned.1.call-start = ((), (), s32[]{:S(2)}) async-start(), calls=%async_computation.7 | async-start | bytes 18874368 | tf_op jit(solution)/shard_map/all_gather | solution.py:176
  11.2 184.5 %all-gather.9.cloned.1.call-start = ((), (), s32[]{:S(2)}) async-start(), calls=%async_computation.8 | async-start | bytes 18874368 | tf_op jit(solution)/shard_map/all_gather | solution.py:176
  103.9 149.6 %all-gather.11.cloned.1.call-start = ((), (), s32[]{:S(2)}) async-start(), calls=%async_computation.9 | async-start | bytes 9437184 | tf_op jit(solution)/shard_map/all_gather | solution.py:190
  108.3 260.7 %copy-start.1 = (s32[256]{0:T(256)S(1)}, s32[256]{0:T(256)}, u32[]{:S(2)}) copy-start(s32[256]{0:T(256)} %param.12) | copy-start | bytes 3076
  195.7 115.6 %all-gather.13.cloned.1.call-start = ((), (), s32[]{:S(2)}) async-start(), calls=%async_computation.10 | async-start | bytes 9437184 | tf_op jit(solution)/shard_map/all_gather | solution.py:190
  253.6 115.4 %all-gather.15.cloned.1.call-start = ((), (), s32[]{:S(2)}) async-start(), calls=%async_computation.11 | async-start | bytes 9437184 | tf_op jit(solution)/shard_map/all_gather | solution.py:190
  311.3 281.7 %all-gather.17.cloned.1.call-start = ((), (), s32[]{:S(2)}) async-start(), calls=%async_computation.12 | async-start | bytes 9437184 | tf_op jit(solution)/shard_map/all_gather | solution.py:190
  370.1 26.4 %all-to-all-start = ((s32[8,1,64]{2,1,0:T(1,128)}), s32[8,1,64]{2,1,0:T(1,128)S(1)}, u32[]{:S(2)}, u32[]{:S(2)}) async-start(s32[8,1,64]{2,1,0:T(1,128)} %sub.31), calls=%async_computation | async-start | bytes 8192 | tf_op jit(solution)/shard_map/all_to_all | solution.py:150
  373.4 12.6 %copy-start.2 = (bf16[256,8192]{1,0:T(8,128)(2,1)S(1)}, bf16[256,8192]{1,0:T(8,128)(2,1)}, u32[]{:S(2)}) copy-start(bf16[256,8192]{1,0:T(8,128)(2,1)} %param.7) | copy-start | bytes 12582916
  394.4 6.3 copy-start.3
  396.5 49.9 %all-to-all-start.1 = ((bf16[8,64,2048]{2,1,0:T(8,128)(2,1)}), bf16[8,64,2048]{2,1,0:T(8,128)(2,1)S(1)}, u32[]{:S(2)}, u32[]{:S(2)}) async-start(bf16[8,64,2048]{2,1,0:T(8,128)(2,1)} %bitcast.4), calls=%async_computation.1 | async-start | bytes 4194304 | tf_op jit(solution)/shard_map/all_to_all | solution.py:194
  446.5 80.8 %slice-start = ((s8[8388608]{0:T(1024)(128)(4,1)}), s8[4194304]{0:T(1024)(128)(4,1)S(1)}, s32[]{:S(2)}) async-start(s8[8388608]{0:T(1024)(128)(4,1)} %bitcast.75), calls=%async_computation.13 | async-start | bytes 8388608
  449.1 78.2 %slice-start.1 = ((s8[8388608]{0:T(1024)(128)(4,1)}), s8[4194304]{0:T(1024)(128)(4,1)S(1)}, s32[]{:S(2)}) async-start(s8[8388608]{0:T(1024)(128)(4,1)} %bitcast.75), calls=%async_computation.14 | async-start | bytes 8388608
  527.2 36.8 %copy-start = (bf16[256,2048]{1,0:T(8,128)(2,1)}, bf16[256,2048]{1,0:T(8,128)(2,1)S(1)}, u32[]{:S(2)}) copy-start(bf16[256,2048]{1,0:T(8,128)(2,1)S(1)} %convolution_convert_fusion.3) | copy-start | bytes 3145732
  530.8 29.7 %all-to-all-start.3 = ((bf16[4,256,512]{2,1,0:T(8,128)(2,1)}), bf16[4,256,512]{2,1,0:T(8,128)(2,1)S(1)}, u32[]{:S(2)}, u32[]{:S(2)}) async-start(bf16[4,256,512]{2,1,0:T(8,128)(2,1)} %pad_maximum_fusion), calls=%async_computation.3 | async-start | bytes 2097152 | tf_op jit(solution)/shard_map/all_to_all | solution.py:222
  560.5 28.7 %all-to-all-start.4 = ((bf16[4,256,512]{2,1,0:T(8,128)(2,1)}), bf16[4,256,512]{2,1,0:T(8,128)(2,1)S(1)}, u32[]{:S(2)}, u32[]{:S(2)}) async-start(bf16[4,256,512]{2,1,0:T(8,128)(2,1)} %pad_maximum_fusion.1), calls=%async_computation.4 | async-start | bytes 2097152 | tf_op jit(solution)/shard_map/all_to_all | solution.py:222
  589.2 28.7 %all-to-all-start.5 = ((bf16[4,256,512]{2,1,0:T(8,128)(2,1)}), bf16[4,256,512]{2,1,0:T(8,128)(2,1)S(1)}, u32[]{:S(2)}, u32[]{:S(2)}) async-start(bf16[4,256,512]{2,1,0:T(8,128)(2,1)} %pad_maximum_fusion.2), calls=%async_computation.5 | async-start | bytes 2097152 | tf_op jit(solution)/shard_map/all_to_all | solution.py:222
  617.9 29.5 %all-to-all-start.6 = ((bf16[4,256,512]{2,1,0:T(8,128)(2,1)}), bf16[4,256,512]{2,1,0:T(8,128)(2,1)}, u32[]{:S(2)}, u32[]{:S(2)}) async-start(bf16[4,256,512]{2,1,0:T(8,128)(2,1)} %pad_maximum_fusion.3), calls=%async_computation.6 | async-start | bytes 2097152 | tf_op jit(solution)/shard_map/all_to_all | solution.py:222
Sparse Core Ops, SparseCore 0:
  11.3 92.5 all-gather.6
  105.8 89.8 all-gather.8
  197.6 55.9 all-gather.10
  255.3 55.9 all-gather.12
  313.0 55.9 all-gather.14
  370.7 74.0 all-gather.16

commit v2 on v1

--- a/solution.py
+++ b/solution.py
@@ -14,8 +14,7 @@
 LANES = 128
 SLOT_TILE = 32
 KEY_TILE = 512
-QUERY_CHUNKS = 2
-OUT_CHUNKS = 4
+OUT_CUTS = (0, 2, 5, 8)
 
 neg_large = -1e30
 
@@ -161,35 +160,24 @@
     )
     valid = sorted_offsets >= 0
 
-    query_parts = []
-    step = head_width // QUERY_CHUNKS
-    gathered = None
-    for c in range(QUERY_CHUNKS):
-        part = w_query[:, c * step : (c + 1) * step]
-        if gathered is not None:
-            part, gathered = lax.optimization_barrier((part, gathered))
-            query_parts.append(
-                jnp.dot(hidden_rows, gathered, preferred_element_type=jnp.float32).astype(
-                    jnp.bfloat16
-                )
-            )
-        gathered = lax.all_gather(part, "row", axis=0, tiled=True)
-    out_parts = []
-    out_step = w_out.shape[1] // OUT_CHUNKS
-    for c in range(OUT_CHUNKS):
-        part = w_out[:, c * out_step : (c + 1) * out_step]
-        if c == 0:
-            part, gathered = lax.optimization_barrier((part, gathered))
-            query_parts.append(
-                jnp.dot(hidden_rows, gathered, preferred_element_type=jnp.float32).astype(
-                    jnp.bfloat16
-                )
-            )
-        else:
-            part, out_parts[-1] = lax.optimization_barrier((part, out_parts[-1]))
-        out_parts.append(lax.all_gather(part, "row", axis=1, tiled=True))
-
-    queries = jnp.concatenate(query_parts, axis=1)
+    columns = jnp.stack(jnp.split(hidden_rows, servers, axis=1))
+    columns = lax.all_to_all(columns, "row", split_axis=0, concat_axis=0, tiled=True)
+    columns = columns.reshape(servers * row_count, w_query.shape[0])
+    bounds = [w_out.shape[1] * cut // 8 for cut in OUT_CUTS]
+    first, *later = [w_out[:, lower:upper] for lower, upper in zip(bounds, bounds[1:])]
+    first = lax.all_gather(first, "row", axis=1, tiled=True)
+    columns, first, route, order, sorted_offsets, starts, valid = lax.optimization_barrier(
+        (columns, first, route, order, sorted_offsets, starts, valid)
+    )
+    shares_sum = lax.psum_scatter(
+        jnp.dot(columns, w_query, preferred_element_type=jnp.float32),
+        "row",
+        scatter_dimension=0,
+        tiled=True,
+    )
+    later, shares_sum = lax.optimization_barrier((tuple(later), shares_sum))
+    out_parts = [first] + [lax.all_gather(part, "row", axis=1, tiled=True) for part in later]
+    queries = shares_sum.astype(jnp.bfloat16)
     outgoing = exact_pick(route, queries)
     incoming = lax.all_to_all(
         outgoing.reshape(servers, capacity, head_width),
@@ -214,15 +202,18 @@
 
     pieces = []
     shares = servers // groups
-    for c in range(OUT_CHUNKS):
+    for part in out_parts:
         partial = jnp.dot(
-            own_rows, out_parts[c], preferred_element_type=jnp.float32
+            own_rows, part, preferred_element_type=jnp.float32
         ).astype(jnp.bfloat16)
-        partial = jnp.stack(jnp.split(partial, groups, axis=1))
-        shared = lax.all_to_all(partial, "tensor", split_axis=0, concat_axis=0, tiled=True)
-        piece = jnp.sum(shared.astype(jnp.float32), axis=0).astype(jnp.bfloat16)
-        pieces.append(piece.reshape(row_count, shares, out_step))
-    return jnp.stack(pieces, axis=2).reshape(row_count, shares * w_out.shape[1])
+        if part is out_parts[-1]:
+            piece = lax.psum_scatter(partial, "tensor", scatter_dimension=1, tiled=True)
+        else:
+            partial = jnp.stack(jnp.split(partial, groups, axis=1))
+            shared = lax.all_to_all(partial, "tensor", split_axis=0, concat_axis=0, tiled=True)
+            piece = jnp.sum(shared.astype(jnp.float32), axis=0).astype(jnp.bfloat16)
+        pieces.append(piece.reshape(row_count, shares, part.shape[1] // servers))
+    return jnp.concatenate(pieces, axis=2).reshape(row_count, shares * w_out.shape[1])
 
 
 def solution(mesh):

time: 660 us -> 516 us (0.78)
  waiting for transfers between devices: 475 us -> 310 us
  blocking collectives: 30 us -> 50.6 us
  local copies, waits for them, and re-layouts: 13 us -> 26.8 us
    all_gather x6 -> x3, waiting for transfers between devices: 353 us -> 26.7 us  [the longest x2 26.7 us: body(): lax.all_gather(part, 'row', axis=1, tiled=True)]
    reduce_scatter x0 -> x2, waiting for transfers between devices: none -> 115 us  [the longest x1 115 us: body(): lax.psum_scatter(jnp.dot(columns, w_query, preferred_element_type=jnp.flo...]
    all_to_all x0 -> x1, waiting for transfers between devices: none -> 69.1 us  [body(): lax.all_to_all(columns, 'row', split_axis=0, concat_axis=0, tiled=True)]
    all_to_all x4 -> x2, waiting for transfers between devices: 78.2 us -> 55.7 us  [body(): lax.all_to_all(partial, 'tensor', split_axis=0, concat_axis=0, tiled=True)]
    all_to_all x1, blocking collectives: 30 us -> 50.6 us  [body(): lax.all_to_all(attended.reshape(servers, capacity, head_width), 'row', sp...]
    unnamed x12 -> x16, local copies, waits for them, and re-layouts: 0.03 us -> 15.6 us
    all_to_all x4 -> x2, starting transfers between devices: 16.1 us -> 9.18 us  [body(): lax.all_to_all(partial, 'tensor', split_axis=0, concat_axis=0, tiled=True)]
    dot_general x6 -> x4, matrix products: 40.8 us -> 34.9 us  [the longest x3 19.8 us: body(): jnp.dot(own_rows, part, preferred_element_type=jnp.float32)]
  transfers between devices with their start and end apart: 12 -> 10, of which waited for: 10 -> 5; matrix products, arithmetic and copies ran while one was open for 10% -> 11% of each run, Pallas kernels for 7% -> 8%
where the time goes in v2:
time: 516 us; the launch traced here: 515 us
  waiting for transfers between devices  310 us (60%)
  blocking collectives  50.6 us (10%)
  matrix products  43.2 us (8%)
  Pallas kernels  41.1 us (8%)
  local copies, waits for them, and re-layouts  26.8 us (5%)
  starting transfers between devices  22.8 us (4%)
  between operations  13.3 us (3%)
  other arithmetic  7.08 us (1%)
    reduce_scatter x1, waiting for transfers between devices, body(): lax.psum_scatter(jnp.dot(columns, w_query, preferred_element_type=jnp.flo...  115 us
    all_to_all x1, waiting for transfers between devices, body(): lax.all_to_all(columns, 'row', split_axis=0, concat_axis=0, tiled=True)  69.1 us
    all_to_all x2, waiting for transfers between devices, body(): lax.all_to_all(partial, 'tensor', split_axis=0, concat_axis=0, tiled=True)  55.7 us
    all_to_all x1, blocking collectives, body(): lax.all_to_all(attended.reshape(servers, capacity, head_width), 'row', sp...  50.6 us
    all_to_all x1, waiting for transfers between devices, body(): lax.all_to_all(outgoing.reshape(servers, capacity, head_width), 'row', sp...  42.6 us
    pallas_call x1, Pallas kernels, attend(): pl.pallas_call(attend_kernel, out_shape=jax.ShapeDtypeStruct((slots, widt...  41.1 us
    all_gather x2, waiting for transfers between devices, body(): lax.all_gather(part, 'row', axis=1, tiled=True)  26.7 us
    dot_general x3, matrix products, body(): jnp.dot(own_rows, part, preferred_element_type=jnp.float32)  19.8 us
  transfers between devices with their start and end apart: 10, of which 5 were waited for; matrix products, arithmetic and copies ran while one was open for 11% of the time, Pallas kernels for 8%

profile of v2, /device:TPU:0, one launch (start us, length us, event | category | flops | bytes accessed | tf_op | source)
XLA Modules:
  0.0 514.8 jit_solution(14160549483309085932)
XLA Ops:
  6.5 2.3 slice.9
  10.5 5.2 %all-to-all-start.1 = ((s32[8,1,64]{2,1,0:T(1,128)}), s32[8,1,64]{2,1,0:T(1,128)S(1)}, u32[]{:S(2)}, u32[]{:S(2)}) async-start(s32[8,1,64]{2,1,0:T(1,128)} %sub.27), calls=%async_computation.1 | async-start | bytes 8192 | tf_op jit(solution)/shard_map/all_to_all | solution.py:149
  15.7 1.9 bitcast_dynamic-update-slice_fusion.7
  17.6 2.0 bitcast_dynamic-update-slice_fusion.6
  19.5 1.9 bitcast_dynamic-update-slice_fusion.5
  21.5 1.9 bitcast_dynamic-update-slice_fusion.4
  23.4 1.9 bitcast_dynamic-update-slice_fusion.3
  25.3 1.9 bitcast_dynamic-update-slice_fusion.2
  27.2 1.9 bitcast_dynamic-update-slice_fusion.1
  29.0 1.9 bitcast_dynamic-update-slice_fusion
  30.9 4.7 all-to-all-start
  38.0 69.1 %all-to-all-done = bf16[8,256,1024]{2,1,0:T(8,128)(2,1)} async-done(((bf16[8,256,1024]{2,1,0:T(8,128)(2,1)}), bf16[8,256,1024]{2,1,0:T(8,128)(2,1)}, u32[]{:S(2)}, u32[]{:S(2)}) %all-to-all-start) | async-done | bytes 4194336 | tf_op jit(solution)/shard_map/all_to_all | solution.py:164
  107.2 15.1 %fusion.5 = f32[2048,2048]{1,0:T(8,128)} fusion(bf16[2048,1024]{1,0:T(8,128)(2,1)} %bitcast.8, bf16[1024,2048]{1,0:T(8,128)(2,1)} %param.8), kind=kOutput, calls=%fused_computation.63 | convolution fusion | flops 8589934592 | bytes 25165824 | tf_op jit(solution)/shard_map/dot_general | solution.py:173
  122.3 3.9 fusion.4
  126.2 115.1 %reduce-scatter.3.cloned.1.call-done = f32[256,2048]{1,0:T(8,128)} async-done(((f32[2048,2048]{1,0:T(8,128)}), f32[256,2048]{1,0:T(8,128)}) %reduce-scatter.3.cloned.1.call-update) | async-done | bytes 2097168 | tf_op jit(solution)/shard_map/reduce_scatter | solution.py:172
  242.9 2.0 convolution_convert_fusion.2
  245.0 3.6 all-to-all-start.2
  249.3 42.6 %all-to-all-done.2 = bf16[8,64,2048]{2,1,0:T(8,128)(2,1)S(1)} async-done(((bf16[8,64,2048]{2,1,0:T(8,128)(2,1)}), bf16[8,64,2048]{2,1,0:T(8,128)(2,1)S(1)}, u32[]{:S(2)}, u32[]{:S(2)}) %all-to-all-start.2) | async-done | bytes 2097184 | tf_op jit(solution)/shard_map/all_to_all | solution.py:182
  291.9 2.6 convolution_convert_fusion.4.q_ref
  294.5 41.1 %attend.1 = bf16[512,2048]{1,0:T(8,128)(2,1)} custom-call(s32[16]{0:T(128)S(1)} %get-tuple-element.40.lo_ref, s32[16]{0:T(128)S(1)} %get-tuple-element.39.hi_ref, bf16[512,2048]{1,0:T(8,128)(2,1)} %convolution_convert_fusion.4.q_ref, bf16[8192,256]{1,0:T(8,128)(2,1)} %k_ref.1, bf16[8192,256]{1,0:T(8,128)(2,1)} %v_ref.1, s32[512,1]{1,0:T(8,128)S(1)} %copy.10.off_ref, ...), custom_call_target="tpu_custom_call" | custom-call | flops 8589934592 | bytes 12582912 | tf_op jit(solution)/shard_map/attend/pallas_call | solution.py:110
  335.6 2.9 convolution_convert_fusion.3
  338.5 50.6 %all_to_all.31 = bf16[8,64,2048]{2,1,0:T(8,128)(2,1)S(1)} all-to-all(bf16[8,64,2048]{2,1,0:T(8,128)(2,1)S(1)} %bitcast.62), channel_id=1, replica_groups=mesh['row'=8,'tensor'=4] {'row'}, dimensions={0} | all-to-all | bytes 4194304 | tf_op jit(solution)/shard_map/all_to_all | solution.py:194
  389.9 2.3 convolution_convert_fusion.6
  392.4 1.1 pad_maximum_fusion.1
  393.5 4.6 all-to-all-start.4
  398.1 9.5 %convolution_convert_fusion = bf16[256,3072]{1,0:T(8,128)(2,1)} fusion(bf16[256,2048]{1,0:T(8,128)(2,1)S(1)} %convolution_convert_fusion.5, bf16[2048,3072]{1,0:T(8,128)(2,1)} %all-gather.8.cloned.1.call-done), kind=kOutput, calls=%fused_computation | convolution fusion | flops 3222011904 | bytes 15204352 | tf_op jit(solution)/shard_map/dot_general | solution.py:206
  407.6 26.7 %all-gather.6.cloned.1.call-done = bf16[2048,3072]{1,0:T(8,128)(2,1)} async-done(((bf16[2048,384]{1,0:T(8,128)(2,1)}), bf16[2048,3072]{1,0:T(8,128)(2,1)}) %all-gather.6.cloned.1.call-update) | async-done | bytes 12582928 | tf_op jit(solution)/shard_map/all_gather | solution.py:179
  434.3 8.0 %convolution_convert_fusion.1 = bf16[256,3072]{1,0:T(8,128)(2,1)S(1)} fusion(bf16[256,2048]{1,0:T(8,128)(2,1)S(1)} %convolution_convert_fusion.5, bf16[2048,3072]{1,0:T(8,128)(2,1)} %all-gather.6.cloned.1.call-done), kind=kOutput, calls=%fused_computation.1 | convolution fusion | flops 3222011904 | bytes 15204352 | tf_op jit(solution)/shard_map/dot_general | solution.py:206
  442.4 1.4 pad_maximum_fusion
  443.8 4.6 all-to-all-start.5
  448.7 55.7 %all-to-all-done.5 = bf16[4,256,768]{2,1,0:T(8,128)(2,1)S(1)} async-done(((bf16[4,256,768]{2,1,0:T(8,128)(2,1)}), bf16[4,256,768]{2,1,0:T(8,128)(2,1)S(1)}, u32[]{:S(2)}, u32[]{:S(2)}) %all-to-all-start.5) | async-done | bytes 1572896 | tf_op jit(solution)/shard_map/all_to_all | solution.py:213
  507.0 1.2 copy.12
  (60 shorter events, 10.4 us)
Async XLA Ops:
  6.5 100.6 %all-gather.4.cloned.1.call-start = ((), (), s32[]{:S(2)}) async-start(), calls=%async_computation.8 | async-start | bytes 9437184 | tf_op jit(solution)/shard_map/all_gather | solution.py:168
  10.5 20.4 %all-to-all-start.1 = ((s32[8,1,64]{2,1,0:T(1,128)}), s32[8,1,64]{2,1,0:T(1,128)S(1)}, u32[]{:S(2)}, u32[]{:S(2)}) async-start(s32[8,1,64]{2,1,0:T(1,128)} %sub.27), calls=%async_computation.1 | async-start | bytes 8192 | tf_op jit(solution)/shard_map/all_to_all | solution.py:149
  30.9 4.7 copy-start.1
  30.9 76.2 %all-to-all-start = ((bf16[8,256,1024]{2,1,0:T(8,128)(2,1)}), bf16[8,256,1024]{2,1,0:T(8,128)(2,1)}, u32[]{:S(2)}, u32[]{:S(2)}) async-start(bf16[8,256,1024]{2,1,0:T(8,128)(2,1)} %bitcast_dynamic-update-slice_fusion), calls=%async_computation | async-start | bytes 8388608 | tf_op jit(solution)/shard_map/all_to_all | solution.py:164
  35.6 205.7 %reduce-scatter.3.cloned.1.call-start = ((), (), s32[]{:S(2)}) async-start(), calls=%async_computation.9 | async-start | bytes 18874368 | tf_op jit(solution)/shard_map/reduce_scatter | solution.py:172
  122.3 275.8 %all-gather.8.cloned.1.call-start = ((), (), s32[]{:S(2)}) async-start(), calls=%async_computation.11 | async-start | bytes 14155776 | tf_op jit(solution)/shard_map/all_gather | solution.py:179
  241.3 1.6 copy-start
  241.3 193.0 %all-gather.6.cloned.1.call-start = ((), (), s32[]{:S(2)}) async-start(), calls=%async_computation.10 | async-start | bytes 14155776 | tf_op jit(solution)/shard_map/all_gather | solution.py:179
  245.0 47.0 %all-to-all-start.2 = ((bf16[8,64,2048]{2,1,0:T(8,128)(2,1)}), bf16[8,64,2048]{2,1,0:T(8,128)(2,1)S(1)}, u32[]{:S(2)}, u32[]{:S(2)}) async-start(bf16[8,64,2048]{2,1,0:T(8,128)(2,1)} %bitcast.11), calls=%async_computation.3 | async-start | bytes 4194304 | tf_op jit(solution)/shard_map/all_to_all | solution.py:182
  291.9 98.0 %slice-start = ((s8[8388608]{0:T(1024)(128)(4,1)}), s8[4194304]{0:T(1024)(128)(4,1)S(1)}, s32[]{:S(2)}) async-start(s8[8388608]{0:T(1024)(128)(4,1)} %bitcast.65), calls=%async_computation.13 | async-start | bytes 8388608
  294.5 95.4 %slice-start.1 = ((s8[8388608]{0:T(1024)(128)(4,1)}), s8[4194304]{0:T(1024)(128)(4,1)S(1)}, s32[]{:S(2)}) async-start(s8[8388608]{0:T(1024)(128)(4,1)} %bitcast.65), calls=%async_computation.14 | async-start | bytes 8388608
  393.5 50.3 %all-to-all-start.4 = ((bf16[4,256,512]{2,1,0:T(8,128)(2,1)}), bf16[4,256,512]{2,1,0:T(8,128)(2,1)S(1)}, u32[]{:S(2)}, u32[]{:S(2)}) async-start(bf16[4,256,512]{2,1,0:T(8,128)(2,1)} %pad_maximum_fusion.1), calls=%async_computation.5 | async-start | bytes 2097152 | tf_op jit(solution)/shard_map/all_to_all | solution.py:213
  398.1 106.9 %reduce-scatter.5.cloned.1.call-start = ((), (), s32[]{:S(2)}) async-start(), calls=%async_computation.12 | async-start | bytes 1966080 | tf_op jit(solution)/shard_map/reduce_scatter | solution.py:210
  443.8 60.6 %all-to-all-start.5 = ((bf16[4,256,768]{2,1,0:T(8,128)(2,1)}), bf16[4,256,768]{2,1,0:T(8,128)(2,1)S(1)}, u32[]{:S(2)}, u32[]{:S(2)}) async-start(bf16[4,256,768]{2,1,0:T(8,128)(2,1)} %pad_maximum_fusion), calls=%async_computation.6 | async-start | bytes 3145728 | tf_op jit(solution)/shard_map/all_to_all | solution.py:213
Sparse Core Ops, SparseCore 0:
  9.2 89.3 all-gather.3
  122.4 118.8 reduce-scatter.2
  243.2 93.8 all-gather.7
  338.8 95.4 all-gather.5
  436.5 52.8 reduce-scatter.4
